TPU v7x, 256 devices: a whole 4x4x8 slice. The times are simulated.
256 devices in a mesh: ctx: 32 (over y_hi, z, core), tp: 8 (over y_lo, x).
Axes of the slice: x: 4, y: 4 (y_hi: 2, y_lo: 2; y = y_hi * 2 + y_lo), z: 8, core: 2. Of those that a mesh axis runs over, the one named last changes fastest.
Arguments:
- query_heads: bfloat16 [4096, 8192], P('ctx', 'tp'), may hold values from -32 to 32
- key_heads: bfloat16 [4096, 8192], P('ctx', 'tp'), may hold values from -6 to 6
- value_heads: bfloat16 [4096, 8192], P('ctx', 'tp'), may hold values from -6 to 6
- hyena_query: bfloat16 [4096, 8192], P('ctx', 'tp'), may hold values from -6 to 6
- hyena_key: bfloat16 [4096, 8192], P('ctx', 'tp'), may hold values from -6 to 6
- hyena_value: bfloat16 [4096, 8192], P('ctx', 'tp'), may hold values from -6 to 6
- short_filter: float32 [3, 7, 8192], P(None, None, 'tp'), may hold values from -2 to 2
- long_filter: float32 [4096, 512], P('ctx', 'tp'), may hold values from -0.09375 to 0.09375
- output_grad: bfloat16 [4096, 8192], P('ctx', 'tp'), may hold values from -70 to 70
Outputs:
- attention: bfloat16 [4096, 8192], P('ctx', 'tp')
- query_grad: bfloat16 [4096, 8192], P('ctx', 'tp')
- key_grad: bfloat16 [4096, 8192], P('ctx', 'tp')
- value_grad: bfloat16 [4096, 8192], P('ctx', 'tp')
- filter_grad: float32 [4096, 512], P('ctx', 'tp')
All inputs are finite; a program needn't handle non-finite values.
Results may differ from a plain program's by a relative error of at most 0.0049.
Values may be sent and summed in bfloat16 or wider, within the bound.
A program may use at most 64 MiB of HBM per device.

v0:
```python
import functools
import math

import jax
import jax.numpy as jnp
from jax import lax
from jax.experimental import pallas as pl
from jax.experimental.pallas import tpu as pltpu
from jax.sharding import PartitionSpec as P

HEAD_DIM = 128
ROWS = 128
CHANNELS = 1024
PEERS = 32
NARROW = 32
GROUP = 16
HELD = 2
TPS = 8
SHORT = 7
RIM = 16
SUPER = 16
LONG = 4096
TOTAL = 4096 * 512
F32 = jnp.float32
BF16 = jnp.bfloat16
MESH = pl.DeviceIdType.MESH


def peer_at(step, me):
    turn = step // 4
    away = ((turn + 1) // 2) * (1 - 2 * (turn % 2)) + 4
    half = 1 - (step // 2) % 2
    core = 1 - step % 2
    return (
        ((me // 16 + half) % 2) * 16 + (((me // 2) % 8 + away) % 8) * 2 + (me % 2 + core) % 2
    )


def dot(a, b, contract):
    return lax.dot_general(a, b, (contract, ((), ())), preferred_element_type=F32)


def kernel(
    q_ref,
    k_ref,
    v_ref,
    hq_ref,
    hk_ref,
    hv_ref,
    taps_ref,
    filt_ref,
    up_ref,
    att_ref,
    qg_ref,
    kg_ref,
    vg_ref,
    fg_ref,
    rim_out,
    rim_in,
    kv_in,
    ext,
    short,
    send_h,
    recv_h,
    send_m,
    recv_m,
    send_g,
    recv_g,
    send_c,
    recv_c,
    send_d,
    recv_d,
    send_f,
    recv_f,
    send_n,
    recv_n,
    edge_out,
    edge_in,
    raw_rows,
    padded_m,
    padded_g,
    left_m,
    left_g,
    weight_c,
    weight_d,
    gram,
    rim_send_sem,
    rim_recv_sem,
    kv_send_sem,
    kv_recv_sem,
    out_sem,
    in_sem,
    edge_send_sem,
    edge_recv_sem,
):
    me = lax.axis_index("ctx")
    tp = lax.axis_index("tp")
    after = (me + 1) % PEERS
    before = (me + PEERS - 1) % PEERS

    barrier = pltpu.get_barrier_semaphore()

    @pl.loop(0, PEERS - 1)
    def _(step):
        pl.semaphore_signal(
            barrier, inc=1, device_id=(peer_at(step, me), tp), device_id_type=MESH
        )

    @pl.loop(1, TPS)
    def _(step):
        pl.semaphore_signal(
            barrier, inc=1, device_id=(me, (tp + step) % TPS), device_id_type=MESH
        )

    rim_out[0:RIM] = hq_ref[ROWS - RIM : ROWS]
    rim_out[RIM : 2 * RIM] = hk_ref[ROWS - RIM : ROWS]
    rim_out[2 * RIM : 3 * RIM] = hv_ref[ROWS - RIM : ROWS]
    filter_first = filt_ref[...].T
    for p in range(PEERS):
        send_h[p] = filter_first[HELD * p : HELD * p + HELD]
    pl.semaphore_wait(barrier, PEERS - 1 + TPS - 1)

    def to_next(src, dst, send_sem, recv_sem, target):
        return pltpu.make_async_remote_copy(
            src_ref=src,
            dst_ref=dst,
            send_sem=send_sem,
            recv_sem=recv_sem,
            device_id=(target, tp),
            device_id_type=MESH,
        )

    rim_copy = to_next(rim_out, rim_in, rim_send_sem, rim_recv_sem, after)
    rim_copy.start()

    def scatter(src, dst, which):
        @pl.loop(0, PEERS - 1)
        def _(step):
            peer = peer_at(step, me)
            to_next(src.at[peer], dst.at[me], out_sem.at[which], in_sem.at[which], peer).start()

        dst[pl.ds(me, 1)] = src[pl.ds(me, 1)]

    def settle(ref, sem):
        part = ref.at[pl.ds(0, PEERS - 1)]
        pltpu.make_async_copy(part, part, sem).wait()

    scatter(send_h, recv_h, 0)
    kv_copies = [
        to_next(src, kv_in.at[n], kv_send_sem.at[n], kv_recv_sem.at[n], after)
        for n, src in enumerate((k_ref, v_ref))
    ]
    for copy in kv_copies:
        copy.start()

    for n, ref in enumerate((hq_ref, hk_ref, hv_ref)):
        ext[n, RIM : RIM + ROWS] = ref[...].astype(F32)
    rim_copy.wait_recv()
    for n in range(3):
        leading = rim_in[n * RIM : (n + 1) * RIM].astype(F32)
        ext[n, 0:RIM] = jnp.where(me > 0, leading, 0.0)

    def short_conv(n, lanes):
        total = taps_ref[n, 0:1, lanes] * ext[n, RIM : RIM + ROWS, lanes]
        for s in range(1, SHORT):
            total += taps_ref[n, s : s + 1, lanes] * ext[n, RIM - s : RIM - s + ROWS, lanes]
        return total

    @pl.loop(0, CHANNELS // 128)
    def _(chunk):
        lanes = pl.ds(pl.multiple_of(chunk * 128, 128), 128)
        short_k = short_conv(1, lanes)
        short_v = short_conv(2, lanes)
        short[1, :, lanes] = short_k
        short[2, :, lanes] = short_v
        mixed = (short_k * short_v).T.astype(BF16)
        send_m[pl.ds(chunk * 4, 4)] = mixed.reshape(4, NARROW, ROWS)

    scatter(send_m, recv_m, 1)

    @pl.loop(0, CHANNELS // 128)
    def _(chunk):
        lanes = pl.ds(pl.multiple_of(chunk * 128, 128), 128)
        delta = (up_ref[:, lanes].astype(F32) * short_conv(0, lanes)).T.astype(BF16)
        send_g[pl.ds(chunk * 4, 4)] = delta.reshape(4, NARROW, ROWS)

    scatter(send_g, recv_g, 2)

    row_at = lax.broadcasted_iota(jnp.int32, (ROWS, ROWS), 0)
    lane_at = lax.broadcasted_iota(jnp.int32, (ROWS, ROWS), 1)
    settle(recv_h, in_sem.at[0])
    zero_tile = jnp.zeros((ROWS, ROWS), BF16)
    for g in range(HELD):
        weight_c[g, 128:256, 0:128] = zero_tile
        weight_d[g, 128:256, 0:128] = zero_tile

        def turned(block, g=g):
            line = jnp.broadcast_to(recv_h[block, g : g + 1], (ROWS, ROWS))
            return pltpu.roll(line, 0, 1, stride=1, stride_axis=0)

        def build(d, last, g=g, turned=turned):
            even = turned(2 * d)
            odd = turned(2 * d + 1)
            tile_even = jnp.where(lane_at >= row_at, even, last).astype(BF16)
            tile_odd = jnp.where(lane_at >= row_at, odd, even).astype(BF16)
            top = pl.multiple_of(d * 256, 256)
            weight_c[g, pl.ds(top, 128), 0:128] = tile_even
            weight_c[g, pl.ds(top + 128, 128), 128:256] = tile_even
            weight_c[g, pl.ds(top, 128), 128:256] = tile_odd
            weight_c[g, pl.ds(top + 384, 128), 0:128] = tile_odd
            weight_d[g, 0:128, pl.ds(top, 128)] = tile_even
            weight_d[g, 128:256, pl.ds(top + 128, 128)] = tile_even
            weight_d[g, 0:128, pl.ds(top + 128, 128)] = tile_odd
            weight_d[g, 128:256, pl.ds(top + 256, 128)] = tile_odd
            return odd

        lax.fori_loop(0, SUPER, build, jnp.zeros((ROWS, ROWS), F32))

    for copy in kv_copies:
        copy.wait_recv()
    query_at = lax.broadcasted_iota(jnp.int32, (ROWS, 2 * ROWS), 0)
    key_at = lax.broadcasted_iota(jnp.int32, (ROWS, 2 * ROWS), 1) - ROWS
    first = jnp.where(me > 0, -ROWS, 0)
    allowed = (key_at <= query_at) & (key_at >= first)

    @pl.loop(0, CHANNELS // HEAD_DIM)
    def _(head):
        lanes = pl.ds(pl.multiple_of(head * HEAD_DIM, HEAD_DIM), HEAD_DIM)
        keys = jnp.concatenate([kv_in[0, :, lanes], k_ref[:, lanes]], 0)
        values = jnp.concatenate([kv_in[1, :, lanes], v_ref[:, lanes]], 0)
        scores = dot(q_ref[:, lanes], keys, ((1,), (1,))) * (1.0 / math.sqrt(HEAD_DIM))
        masked = jnp.where(allowed, scores, -jnp.inf)
        largest = jnp.max(masked, axis=1, keepdims=True)
        raised = jnp.exp(masked - largest)
        weights = (raised / jnp.sum(raised, axis=1, keepdims=True)).astype(BF16)
        att_ref[:, lanes] = dot(weights, values, ((1,), (0,))).astype(BF16)

    half = SUPER * GROUP

    def paired(recv, g):
        rows = recv[:, g * GROUP : (g + 1) * GROUP, :].reshape(SUPER, 2, GROUP, ROWS)
        return rows[:, 0].reshape(half, ROWS), rows[:, 1].reshape(half, ROWS)

    def spread(send, result, g):
        both = jnp.stack(
            [
                result[:, 0:ROWS].reshape(SUPER, GROUP, ROWS),
                result[:, ROWS : 2 * ROWS].reshape(SUPER, GROUP, ROWS),
            ],
            axis=1,
        )
        send[:, g * GROUP : (g + 1) * GROUP, :] = both.reshape(PEERS, GROUP, ROWS)

    settle(recv_m, in_sem.at[1])
    padded_m[0:half] = jnp.zeros((half, 2 * ROWS), BF16)
    for g in range(HELD):
        even, odd = paired(recv_m, g)
        padded_m[half : 2 * half, 0:ROWS] = even
        padded_m[half : 2 * half, ROWS : 2 * ROWS] = odd
        for d in range(SUPER):
            left_m[:, d * 256 : (d + 1) * 256] = padded_m[half - GROUP * d : 2 * half - GROUP * d]
        conv = dot(left_m[...], weight_c[g, 0:LONG], ((1,), (0,))).astype(BF16)
        spread(send_c, conv, g)
    scatter(send_c, recv_c, 3)

    settle(recv_g, in_sem.at[2])
    padded_g[half : 2 * half] = jnp.zeros((half, 2 * ROWS), BF16)
    for g in range(HELD):
        even, odd = paired(recv_g, g)
        padded_g[0:half, 0:ROWS] = even
        padded_g[0:half, ROWS : 2 * ROWS] = odd
        for d in range(SUPER):
            left_g[g, :, d * 256 : (d + 1) * 256] = padded_g[GROUP * d : half + GROUP * d]
        back = dot(left_g[g], weight_d[g, :, 0:LONG], ((1,), (1,))).astype(BF16)
        spread(send_d, back, g)
    scatter(send_d, recv_d, 4)

    reversal = (row_at + lane_at == ROWS - 1).astype(BF16)
    upper = (lane_at < row_at) | (lane_at == ROWS - 1)
    for g in range(HELD):
        turned_m = jnp.concatenate(
            [dot(reversal, part, ((1,), (1,))).astype(BF16) for part in paired(recv_m, g)], 0
        )
        gram[:, 0:LONG] = dot(turned_m, left_g[g], ((1,), (0,)))
        gram[:, LONG : LONG + ROWS] = jnp.zeros((2 * ROWS, ROWS), F32)

        @pl.loop(0, PEERS)
        def _(e, g=g):
            at = pl.multiple_of(e * ROWS, ROWS)
            tile = gram[0:ROWS, pl.ds(at, ROWS)] + gram[ROWS : 2 * ROWS, pl.ds(at + ROWS, ROWS)]
            slid = pltpu.roll(tile, 0, 1, stride=1, stride_axis=0)
            raw_rows[0, pl.ds(e, 1)] = jnp.sum(jnp.where(upper, slid, 0.0), 0, keepdims=True)
            raw_rows[1, pl.ds(e, 1)] = jnp.sum(jnp.where(upper, 0.0, slid), 0, keepdims=True)

        raw_rows[1, PEERS : PEERS + 8] = jnp.zeros((8, ROWS), F32)
        raw = raw_rows[0, 0:PEERS] + raw_rows[1, 1 : PEERS + 1]
        raw = pltpu.roll(raw, 1, 1)
        squares = jnp.sum(raw * raw, 0, keepdims=True)
        send_f[:, g : g + 1, :] = raw.reshape(PEERS, 1, ROWS)
        send_f[:, HELD + g : HELD + g + 1, :] = jnp.broadcast_to(
            squares.reshape(1, 1, ROWS), (PEERS, 1, ROWS)
        )
    scatter(send_f, recv_f, 5)

    def follow(n, source):
        def chunk_step(chunk, carry):
            lanes = pl.ds(pl.multiple_of(chunk * 128, 128), 128)
            part = source[pl.ds(chunk * 4, 4)].reshape(4 * NARROW, ROWS).astype(F32).T
            if n == 0:
                grads = ((0, up_ref[:, lanes].astype(F32) * part),)
            else:
                grads = ((1, part * short[2, :, lanes]), (2, part * short[1, :, lanes]))
            for which, grad in grads:
                ext[which, 0:ROWS, lanes] = grad
                edge_out[which, :, lanes] = grad[0:RIM].astype(BF16)
            return carry

        lax.fori_loop(0, CHANNELS // 128, chunk_step, 0)

    def edge_copy(n):
        part = pl.ds(0, 1) if n == 0 else pl.ds(1, 2)
        return to_next(
            edge_out.at[part],
            edge_in.at[part],
            edge_send_sem.at[n],
            edge_recv_sem.at[n],
            before,
        )

    def anti_short(n, out):
        trailing = edge_in[n].astype(F32)
        ext[n, ROWS : ROWS + RIM] = jnp.where(me < PEERS - 1, trailing, 0.0)

        @pl.loop(0, CHANNELS // 128)
        def _(chunk):
            lanes = pl.ds(pl.multiple_of(chunk * 128, 128), 128)
            total = taps_ref[n, 0:1, lanes] * ext[n, 0:ROWS, lanes]
            for s in range(1, SHORT):
                total += taps_ref[n, s : s + 1, lanes] * ext[n, s : s + ROWS, lanes]
            out[:, lanes] = total.astype(BF16)

    settle(recv_c, in_sem.at[3])
    follow(0, recv_c)
    edge_copy(0).start()
    settle(recv_d, in_sem.at[4])
    follow(1, recv_d)
    edge_copy(1).start()

    settle(recv_f, in_sem.at[5])
    squares = jnp.sum(recv_f[:, HELD : 2 * HELD, :], axis=0)
    squares = jnp.sum(squares, axis=0, keepdims=True)
    send_n[...] = jnp.broadcast_to(squares, (8, ROWS))

    def norm_copy(step):
        return pltpu.make_async_remote_copy(
            src_ref=send_n,
            dst_ref=recv_n.at[tp],
            send_sem=out_sem.at[6],
            recv_sem=in_sem.at[6],
            device_id=(me, (tp + step) % TPS),
            device_id_type=MESH,
        )

    @pl.loop(1, TPS)
    def _(step):
        norm_copy(step).start()

    recv_n[pl.ds(tp, 1)] = send_n[...].reshape(1, 8, ROWS)

    edge_copy(0).wait_recv()
    anti_short(0, qg_ref)
    edge_copy(1).wait_recv()
    anti_short(1, kg_ref)
    anti_short(2, vg_ref)

    part = recv_n.at[pl.ds(0, TPS - 1)]
    pltpu.make_async_copy(part, part, in_sem.at[6]).wait()
    total = jnp.sum(recv_n[:, 0, :], axis=0, keepdims=True)
    total = jnp.sum(total, axis=1, keepdims=True)
    factor = jnp.minimum(1.0, math.sqrt(TOTAL) / jnp.sqrt(total))
    rows = jnp.concatenate([recv_f[p, 0:HELD] for p in range(PEERS)], 0)
    fg_ref[...] = (rows * factor).T

    rim_copy.wait_send()
    for copy in kv_copies:
        copy.wait_send()
    for n in range(2):
        edge_copy(n).wait_send()
    for n, ref in enumerate((send_h, send_m, send_g, send_c, send_d, send_f)):
        settle(ref, out_sem.at[n])
    pltpu.make_async_copy(part, part, out_sem.at[6]).wait()


def on_device(*args):
    vmem = pl.BlockSpec(memory_space=pltpu.VMEM)
    wide = jax.ShapeDtypeStruct((ROWS, CHANNELS), BF16)
    exchanged = pltpu.VMEM((PEERS, NARROW, ROWS), BF16)
    half = SUPER * GROUP
    return pl.pallas_call(
        kernel,
        out_shape=(wide, wide, wide, wide, jax.ShapeDtypeStruct((ROWS, 64), F32)),
        in_specs=[vmem] * 9,
        out_specs=(vmem,) * 5,
        scratch_shapes=[
            pltpu.VMEM((3 * RIM, CHANNELS), BF16),
            pltpu.VMEM((3 * RIM, CHANNELS), BF16),
            pltpu.VMEM((2, ROWS, CHANNELS), BF16),
            pltpu.VMEM((3, ROWS + RIM, CHANNELS), F32),
            pltpu.VMEM((3, ROWS, CHANNELS), F32),
            pltpu.VMEM((PEERS, HELD, ROWS), F32),
            pltpu.VMEM((PEERS, HELD, ROWS), F32),
            *[exchanged] * 8,
            pltpu.VMEM((PEERS, 2 * HELD, ROWS), F32),
            pltpu.VMEM((PEERS, 2 * HELD, ROWS), F32),
            pltpu.VMEM((8, ROWS), F32),
            pltpu.VMEM((TPS, 8, ROWS), F32),
            pltpu.VMEM((3, RIM, CHANNELS), BF16),
            pltpu.VMEM((3, RIM, CHANNELS), BF16),
            pltpu.VMEM((2, PEERS + 8, ROWS), F32),
            pltpu.VMEM((2 * half, 2 * ROWS), BF16),
            pltpu.VMEM((2 * half, 2 * ROWS), BF16),
            pltpu.VMEM((half, LONG), BF16),
            pltpu.VMEM((HELD, half, LONG), BF16),
            pltpu.VMEM((HELD, LONG + 256, 256), BF16),
            pltpu.VMEM((HELD, 256, LONG + 128), BF16),
            pltpu.VMEM((2 * ROWS, LONG + ROWS), F32),
            pltpu.SemaphoreType.DMA,
            pltpu.SemaphoreType.DMA,
            pltpu.SemaphoreType.DMA((2,)),
            pltpu.SemaphoreType.DMA((2,)),
            pltpu.SemaphoreType.DMA((7,)),
            pltpu.SemaphoreType.DMA((7,)),
            pltpu.SemaphoreType.DMA((2,)),
            pltpu.SemaphoreType.DMA((2,)),
        ],
        compiler_params=pltpu.CompilerParams(
            collective_id=0, has_side_effects=True, vmem_limit_bytes=56 * 1024 * 1024
        ),
        cost_estimate=pl.CostEstimate(
            flops=3_400_000_000, bytes_accessed=4_000_000, transcendentals=300_000
        ),
    )(*args)


def solution(mesh):
    wide = P("ctx", "tp")
    in_specs = (wide,) * 6 + (P(None, None, "tp"), wide, wide)
    return jax.shard_map(
        on_device, mesh=mesh, in_specs=in_specs, out_specs=(wide,) * 5, check_vma=False
    )
```

profile of v0, /device:TPU:1, one launch (start us, length us, event | category | flops | bytes accessed | tf_op | source)
XLA Modules:
  0.0 64.5 jit_solution(5662812227259849757)
XLA Ops:
  0.6 1.5 %copy.14.filt_ref = f32[128,64]{1,0:T(8,128)} copy(f32[128,64]{0,1:T(8,128)} %param.16) | data formatting | bytes 65536 | tf_op args[7]
  2.1 56.3 %shard_map.128 = (bf16[128,1024]{1,0:T(8,128)(2,1)}, bf16[128,1024]{1,0:T(8,128)(2,1)}, bf16[128,1024]{1,0:T(8,128)(2,1)}, bf16[128,1024]{1,0:T(8,128)(2,1)}, f32[128,64]{1,0:T(8,128)}) custom-call(bf16[128,1024]{1,0:T(8,128)(2,1)} %q_ref.1, bf16[128,1024]{1,0:T(8,128)(2,1)} %k_ref.1, bf16[128,1024]{1,0:T(8,128)(2,1)} %v_ref.1, bf16[128,1024]{1,0:T(8,128)(2,1)} %hq_ref.1, ...), custom_call_target="tpu_custom_call" | custom-call | flops 3400000000 | bytes 4000000 | tf_op jit(solution)/shard_map/pallas_call | solution.py:399
  58.4 1.5 %copy.15 = f32[128,64]{0,1:T(8,128)} copy(f32[128,64]{1,0:T(8,128)} %get-tuple-element.9) | data formatting | bytes 65536 | tf_op jit(solution)/shard_map/pallas_call | solution.py:399
  60.0 0.0 copy-start.2
  60.0 1.7 %copy.20 = bf16[128,1024]{1,0:T(8,128)(2,1)} copy(bf16[128,1024]{1,0:T(8,128)(2,1)} %get-tuple-element.15) | data formatting | bytes 524288
  61.7 0.0 copy-done.2
  61.7 0.0 copy-start.1
  61.7 0.7 %copy.21 = bf16[128,1024]{1,0:T(8,128)(2,1)} copy(bf16[128,1024]{1,0:T(8,128)(2,1)S(1)} %copy-done.2) | data formatting | bytes 524288
  62.4 0.3 copy-done.1
  62.7 0.0 copy-start
  62.7 0.7 %copy.22 = bf16[128,1024]{1,0:T(8,128)(2,1)} copy(bf16[128,1024]{1,0:T(8,128)(2,1)S(1)} %copy-done.1) | data formatting | bytes 524288
  63.4 0.3 copy-done
  63.8 0.7 %copy.23 = bf16[128,1024]{1,0:T(8,128)(2,1)} copy(bf16[128,1024]{1,0:T(8,128)(2,1)S(1)} %copy-done) | data formatting | bytes 524288
Async XLA Ops:
  60.0 1.7 %copy-start.2 = (bf16[128,1024]{1,0:T(8,128)(2,1)S(1)}, bf16[128,1024]{1,0:T(8,128)(2,1)}, u32[]{:S(2)}) copy-start(bf16[128,1024]{1,0:T(8,128)(2,1)} %get-tuple-element.16) | copy-start | bytes 786436
  61.7 1.0 %copy-start.1 = (bf16[128,1024]{1,0:T(8,128)(2,1)S(1)}, bf16[128,1024]{1,0:T(8,128)(2,1)}, u32[]{:S(2)}) copy-start(bf16[128,1024]{1,0:T(8,128)(2,1)} %get-tuple-element.17) | copy-start | bytes 786436
  62.7 1.0 %copy-start = (bf16[128,1024]{1,0:T(8,128)(2,1)S(1)}, bf16[128,1024]{1,0:T(8,128)(2,1)}, u32[]{:S(2)}) copy-start(bf16[128,1024]{1,0:T(8,128)(2,1)} %get-tuple-element.18) | copy-start | bytes 786436
where the time goes:
time: 64.8 us; the launch traced here: 64.5 us
  Pallas kernels  56.3 us (87%)
  local copies, waits for them, and re-layouts  7.53 us (12%)
    pallas_call x1, Pallas kernels, on_device(): pl.pallas_call(kernel, out_shape=(wide, wide, wide, wide, jax.ShapeDtypeS...  56.3 us
    unnamed x11, local copies, waits for them, and re-layouts  5.99 us
    pallas_call x1, local copies, waits for them, and re-layouts, on_device(): pl.pallas_call(kernel, out_shape=(wide, wide, wide, wide, jax.ShapeDtypeS...  1.54 us

commit v1 on v0

--- a/solution.py
+++ b/solution.py
@@ -26,14 +26,9 @@
 MESH = pl.DeviceIdType.MESH
 
 
-def peer_at(step, me):
-    turn = step // 4
-    away = ((turn + 1) // 2) * (1 - 2 * (turn % 2)) + 4
-    half = 1 - (step // 2) % 2
-    core = 1 - step % 2
-    return (
-        ((me // 16 + half) % 2) * 16 + (((me // 2) % 8 + away) % 8) * 2 + (me % 2 + core) % 2
-    )
+STEPS = (8, 24, 7, 25, 9, 23, 6, 26, 10, 22, 5, 27, 11, 21, 4, 28)
+STEPS += (12, 20, 3, 29, 13, 19, 2, 30, 14, 18, 1, 31, 15, 17, 16)
+INPUTS = 9
 
 
 def dot(a, b, contract):
@@ -41,6 +36,20 @@
 
 
 def kernel(
+    q_hbm,
+    k_hbm,
+    v_hbm,
+    hq_hbm,
+    hk_hbm,
+    hv_hbm,
+    taps_hbm,
+    filt_hbm,
+    up_hbm,
+    att_ref,
+    qg_ref,
+    ext,
+    raw_ref,
+    factor_ref,
     q_ref,
     k_ref,
     v_ref,
@@ -50,15 +59,10 @@
     taps_ref,
     filt_ref,
     up_ref,
-    att_ref,
-    qg_ref,
-    kg_ref,
-    vg_ref,
-    fg_ref,
+    load_sem,
     rim_out,
     rim_in,
     kv_in,
-    ext,
     short,
     send_h,
     recv_h,
@@ -93,6 +97,7 @@
     edge_send_sem,
     edge_recv_sem,
 ):
+    hbm = (q_hbm, k_hbm, v_hbm, hq_hbm, hk_hbm, hv_hbm, filt_hbm, up_hbm, taps_hbm)
     me = lax.axis_index("ctx")
     tp = lax.axis_index("tp")
     after = (me + 1) % PEERS
@@ -100,24 +105,32 @@
 
     barrier = pltpu.get_barrier_semaphore()
 
-    @pl.loop(0, PEERS - 1)
-    def _(step):
+    held = (q_ref, k_ref, v_ref, hq_ref, hk_ref, hv_ref, filt_ref, up_ref, taps_ref)
+    loads = [pltpu.make_async_copy(hbm[n], held[n], load_sem.at[n]) for n in range(INPUTS)]
+    for n in (3, 4, 5, 6, 1, 2, 8, 7, 0):
+        loads[n].start()
+
+    for step in STEPS:
         pl.semaphore_signal(
-            barrier, inc=1, device_id=(peer_at(step, me), tp), device_id_type=MESH
-        )
-
-    @pl.loop(1, TPS)
-    def _(step):
+            barrier, inc=1, device_id=((me + step) % PEERS, tp), device_id_type=MESH
+        )
+    for step in range(1, TPS):
         pl.semaphore_signal(
             barrier, inc=1, device_id=(me, (tp + step) % TPS), device_id_type=MESH
         )
 
+    for n in (3, 4, 5):
+        loads[n].wait()
     rim_out[0:RIM] = hq_ref[ROWS - RIM : ROWS]
     rim_out[RIM : 2 * RIM] = hk_ref[ROWS - RIM : ROWS]
     rim_out[2 * RIM : 3 * RIM] = hv_ref[ROWS - RIM : ROWS]
-    filter_first = filt_ref[...].T
+    for n in range(3):
+        ext[n, RIM : RIM + ROWS] = held[3 + n][...].astype(F32)
+    loads[6].wait()
     for p in range(PEERS):
-        send_h[p] = filter_first[HELD * p : HELD * p + HELD]
+        send_h[p] = filt_ref[HELD * p : HELD * p + HELD]
+    loads[1].wait()
+    loads[2].wait()
     pl.semaphore_wait(barrier, PEERS - 1 + TPS - 1)
 
     def to_next(src, dst, send_sem, recv_sem, target):
@@ -133,28 +146,29 @@
     rim_copy = to_next(rim_out, rim_in, rim_send_sem, rim_recv_sem, after)
     rim_copy.start()
 
+    def send_one(src, dst, which, peer):
+        to_next(src.at[peer], dst.at[me], out_sem.at[which], in_sem.at[which], peer).start()
+
+    def keep(src, dst):
+        dst[pl.ds(me, 1)] = src[pl.ds(me, 1)]
+
     def scatter(src, dst, which):
-        @pl.loop(0, PEERS - 1)
-        def _(step):
-            peer = peer_at(step, me)
-            to_next(src.at[peer], dst.at[me], out_sem.at[which], in_sem.at[which], peer).start()
-
-        dst[pl.ds(me, 1)] = src[pl.ds(me, 1)]
+        for step in STEPS:
+            send_one(src, dst, which, (me + step) % PEERS)
+        keep(src, dst)
 
     def settle(ref, sem):
         part = ref.at[pl.ds(0, PEERS - 1)]
         pltpu.make_async_copy(part, part, sem).wait()
 
-    scatter(send_h, recv_h, 0)
     kv_copies = [
         to_next(src, kv_in.at[n], kv_send_sem.at[n], kv_recv_sem.at[n], after)
         for n, src in enumerate((k_ref, v_ref))
     ]
     for copy in kv_copies:
         copy.start()
-
-    for n, ref in enumerate((hq_ref, hk_ref, hv_ref)):
-        ext[n, RIM : RIM + ROWS] = ref[...].astype(F32)
+    scatter(send_h, recv_h, 0)
+
     rim_copy.wait_recv()
     for n in range(3):
         leading = rim_in[n * RIM : (n + 1) * RIM].astype(F32)
@@ -166,8 +180,25 @@
             total += taps_ref[n, s : s + 1, lanes] * ext[n, RIM - s : RIM - s + ROWS, lanes]
         return total
 
-    @pl.loop(0, CHANNELS // 128)
-    def _(chunk):
+    mine = me // 4
+
+    def by_chunk(compute, src, dst, which):
+        def chunk_at(step):
+            return (mine + 4 + ((step + 1) // 2) * (1 - 2 * (step % 2))) % 8
+
+        @pl.loop(0, 7)
+        def _(step):
+            chunk = chunk_at(step)
+            compute(chunk)
+            for n in range(4):
+                send_one(src, dst, which, chunk * 4 + n)
+
+        compute(mine)
+        for n in range(1, 4):
+            send_one(src, dst, which, mine * 4 + (me + n) % 4)
+        keep(src, dst)
+
+    def mixed_chunk(chunk):
         lanes = pl.ds(pl.multiple_of(chunk * 128, 128), 128)
         short_k = short_conv(1, lanes)
         short_v = short_conv(2, lanes)
@@ -176,34 +207,35 @@
         mixed = (short_k * short_v).T.astype(BF16)
         send_m[pl.ds(chunk * 4, 4)] = mixed.reshape(4, NARROW, ROWS)
 
-    scatter(send_m, recv_m, 1)
-
-    @pl.loop(0, CHANNELS // 128)
-    def _(chunk):
+    def delta_chunk(chunk):
         lanes = pl.ds(pl.multiple_of(chunk * 128, 128), 128)
         delta = (up_ref[:, lanes].astype(F32) * short_conv(0, lanes)).T.astype(BF16)
         send_g[pl.ds(chunk * 4, 4)] = delta.reshape(4, NARROW, ROWS)
 
-    scatter(send_g, recv_g, 2)
+    loads[8].wait()
+    by_chunk(mixed_chunk, send_m, recv_m, 1)
+    loads[7].wait()
+    by_chunk(delta_chunk, send_g, recv_g, 2)
 
     row_at = lax.broadcasted_iota(jnp.int32, (ROWS, ROWS), 0)
     lane_at = lax.broadcasted_iota(jnp.int32, (ROWS, ROWS), 1)
     settle(recv_h, in_sem.at[0])
-    zero_tile = jnp.zeros((ROWS, ROWS), BF16)
     for g in range(HELD):
-        weight_c[g, 128:256, 0:128] = zero_tile
-        weight_d[g, 128:256, 0:128] = zero_tile
-
-        def turned(block, g=g):
-            line = jnp.broadcast_to(recv_h[block, g : g + 1], (ROWS, ROWS))
-            return pltpu.roll(line, 0, 1, stride=1, stride_axis=0)
-
-        def build(d, last, g=g, turned=turned):
-            even = turned(2 * d)
-            odd = turned(2 * d + 1)
-            tile_even = jnp.where(lane_at >= row_at, even, last).astype(BF16)
+        weight_c[g, 128:256, 0:128] = jnp.zeros((ROWS, ROWS), BF16)
+        weight_d[g, 128:256, 0:128] = jnp.zeros((ROWS, ROWS), BF16)
+
+    def turned(block, g):
+        line = jnp.broadcast_to(recv_h[block, g : g + 1], (ROWS, ROWS))
+        return pltpu.roll(line, 0, 1, stride=1, stride_axis=0)
+
+    def build(d, last):
+        top = pl.multiple_of(d * 256, 256)
+        carried = []
+        for g in range(HELD):
+            even = turned(2 * d, g)
+            odd = turned(2 * d + 1, g)
+            tile_even = jnp.where(lane_at >= row_at, even, last[g]).astype(BF16)
             tile_odd = jnp.where(lane_at >= row_at, odd, even).astype(BF16)
-            top = pl.multiple_of(d * 256, 256)
             weight_c[g, pl.ds(top, 128), 0:128] = tile_even
             weight_c[g, pl.ds(top + 128, 128), 128:256] = tile_even
             weight_c[g, pl.ds(top, 128), 128:256] = tile_odd
@@ -212,28 +244,10 @@
             weight_d[g, 128:256, pl.ds(top + 128, 128)] = tile_even
             weight_d[g, 0:128, pl.ds(top + 128, 128)] = tile_odd
             weight_d[g, 128:256, pl.ds(top + 256, 128)] = tile_odd
-            return odd
-
-        lax.fori_loop(0, SUPER, build, jnp.zeros((ROWS, ROWS), F32))
-
-    for copy in kv_copies:
-        copy.wait_recv()
-    query_at = lax.broadcasted_iota(jnp.int32, (ROWS, 2 * ROWS), 0)
-    key_at = lax.broadcasted_iota(jnp.int32, (ROWS, 2 * ROWS), 1) - ROWS
-    first = jnp.where(me > 0, -ROWS, 0)
-    allowed = (key_at <= query_at) & (key_at >= first)
-
-    @pl.loop(0, CHANNELS // HEAD_DIM)
-    def _(head):
-        lanes = pl.ds(pl.multiple_of(head * HEAD_DIM, HEAD_DIM), HEAD_DIM)
-        keys = jnp.concatenate([kv_in[0, :, lanes], k_ref[:, lanes]], 0)
-        values = jnp.concatenate([kv_in[1, :, lanes], v_ref[:, lanes]], 0)
-        scores = dot(q_ref[:, lanes], keys, ((1,), (1,))) * (1.0 / math.sqrt(HEAD_DIM))
-        masked = jnp.where(allowed, scores, -jnp.inf)
-        largest = jnp.max(masked, axis=1, keepdims=True)
-        raised = jnp.exp(masked - largest)
-        weights = (raised / jnp.sum(raised, axis=1, keepdims=True)).astype(BF16)
-        att_ref[:, lanes] = dot(weights, values, ((1,), (0,))).astype(BF16)
+            carried.append(odd)
+        return tuple(carried)
+
+    lax.fori_loop(0, SUPER, build, (jnp.zeros((ROWS, ROWS), F32),) * HELD)
 
     half = SUPER * GROUP
 
@@ -282,25 +296,52 @@
             [dot(reversal, part, ((1,), (1,))).astype(BF16) for part in paired(recv_m, g)], 0
         )
         gram[:, 0:LONG] = dot(turned_m, left_g[g], ((1,), (0,)))
-        gram[:, LONG : LONG + ROWS] = jnp.zeros((2 * ROWS, ROWS), F32)
-
-        @pl.loop(0, PEERS)
-        def _(e, g=g):
+        gram[:, LONG : LONG + 2 * ROWS] = jnp.zeros((2 * ROWS, 2 * ROWS), F32)
+
+        def slid(e):
             at = pl.multiple_of(e * ROWS, ROWS)
             tile = gram[0:ROWS, pl.ds(at, ROWS)] + gram[ROWS : 2 * ROWS, pl.ds(at + ROWS, ROWS)]
-            slid = pltpu.roll(tile, 0, 1, stride=1, stride_axis=0)
-            raw_rows[0, pl.ds(e, 1)] = jnp.sum(jnp.where(upper, slid, 0.0), 0, keepdims=True)
-            raw_rows[1, pl.ds(e, 1)] = jnp.sum(jnp.where(upper, 0.0, slid), 0, keepdims=True)
-
-        raw_rows[1, PEERS : PEERS + 8] = jnp.zeros((8, ROWS), F32)
-        raw = raw_rows[0, 0:PEERS] + raw_rows[1, 1 : PEERS + 1]
-        raw = pltpu.roll(raw, 1, 1)
+            return pltpu.roll(tile, 0, 1, stride=1, stride_axis=0)
+
+        @pl.loop(0, PEERS // 4)
+        def _(quad, slid=slid):
+            tiles = [slid(quad * 4 + n) for n in range(5)]
+            for n in range(4):
+                merged = jnp.where(upper, tiles[n], tiles[n + 1])
+                raw_rows[quad * 4 + n] = jnp.sum(merged.reshape(16, 8, ROWS), axis=0)
+
+        raw = pltpu.roll(jnp.sum(raw_rows[...], axis=1), 1, 1)
         squares = jnp.sum(raw * raw, 0, keepdims=True)
         send_f[:, g : g + 1, :] = raw.reshape(PEERS, 1, ROWS)
         send_f[:, HELD + g : HELD + g + 1, :] = jnp.broadcast_to(
             squares.reshape(1, 1, ROWS), (PEERS, 1, ROWS)
         )
     scatter(send_f, recv_f, 5)
+
+    for copy in kv_copies:
+        copy.wait_recv()
+    query_at = lax.broadcasted_iota(jnp.int32, (ROWS, 2 * ROWS), 0)
+    key_at = lax.broadcasted_iota(jnp.int32, (ROWS, 2 * ROWS), 1) - ROWS
+    first = jnp.where(me > 0, -ROWS, 0)
+    allowed = (key_at <= query_at) & (key_at >= first)
+
+    loads[0].wait()
+
+    def attend(head):
+        lanes = pl.ds(pl.multiple_of(head * HEAD_DIM, HEAD_DIM), HEAD_DIM)
+        keys = jnp.concatenate([kv_in[0, :, lanes], k_ref[:, lanes]], 0)
+        values = jnp.concatenate([kv_in[1, :, lanes], v_ref[:, lanes]], 0)
+        scores = dot(q_ref[:, lanes], keys, ((1,), (1,))) * (1.0 / math.sqrt(HEAD_DIM))
+        masked = jnp.where(allowed, scores, -jnp.inf)
+        largest = jnp.max(masked, axis=1, keepdims=True)
+        raised = jnp.exp(masked - largest)
+        weights = (raised / jnp.sum(raised, axis=1, keepdims=True)).astype(BF16)
+        att_ref[:, lanes] = dot(weights, values, ((1,), (0,))).astype(BF16)
+
+    @pl.loop(0, CHANNELS // HEAD_DIM // 2)
+    def _(pair):
+        attend(2 * pair)
+        attend(2 * pair + 1)
 
     def follow(n, source):
         def chunk_step(chunk, carry):
@@ -327,21 +368,21 @@
             before,
         )
 
-    def anti_short(n, out):
+    def trail(n):
         trailing = edge_in[n].astype(F32)
         ext[n, ROWS : ROWS + RIM] = jnp.where(me < PEERS - 1, trailing, 0.0)
-
-        @pl.loop(0, CHANNELS // 128)
-        def _(chunk):
-            lanes = pl.ds(pl.multiple_of(chunk * 128, 128), 128)
-            total = taps_ref[n, 0:1, lanes] * ext[n, 0:ROWS, lanes]
-            for s in range(1, SHORT):
-                total += taps_ref[n, s : s + 1, lanes] * ext[n, s : s + ROWS, lanes]
-            out[:, lanes] = total.astype(BF16)
 
     settle(recv_c, in_sem.at[3])
     follow(0, recv_c)
     edge_copy(0).start()
+    edge_copy(0).wait_recv()
+    trail(0)
+
+    @pl.loop(0, CHANNELS // 128)
+    def _(chunk):
+        lanes = pl.ds(pl.multiple_of(chunk * 128, 128), 128)
+        qg_ref[:, lanes] = anti_short(ext, taps_ref, 0, lanes)
+
     settle(recv_d, in_sem.at[4])
     follow(1, recv_d)
     edge_copy(1).start()
@@ -367,19 +408,18 @@
 
     recv_n[pl.ds(tp, 1)] = send_n[...].reshape(1, 8, ROWS)
 
-    edge_copy(0).wait_recv()
-    anti_short(0, qg_ref)
+    for p in range(PEERS):
+        raw_ref[HELD * p : HELD * p + HELD] = recv_f[p, 0:HELD]
     edge_copy(1).wait_recv()
-    anti_short(1, kg_ref)
-    anti_short(2, vg_ref)
+    trail(1)
+    trail(2)
 
     part = recv_n.at[pl.ds(0, TPS - 1)]
     pltpu.make_async_copy(part, part, in_sem.at[6]).wait()
     total = jnp.sum(recv_n[:, 0, :], axis=0, keepdims=True)
     total = jnp.sum(total, axis=1, keepdims=True)
     factor = jnp.minimum(1.0, math.sqrt(TOTAL) / jnp.sqrt(total))
-    rows = jnp.concatenate([recv_f[p, 0:HELD] for p in range(PEERS)], 0)
-    fg_ref[...] = (rows * factor).T
+    factor_ref[...] = jnp.broadcast_to(factor, (8, ROWS))
 
     rim_copy.wait_send()
     for copy in kv_copies:
@@ -391,21 +431,89 @@
     pltpu.make_async_copy(part, part, out_sem.at[6]).wait()
 
 
+def anti_short(ext, taps_ref, n, lanes):
+    total = taps_ref[n, 0:1, lanes] * ext[n, 0:ROWS, lanes]
+    for s in range(1, SHORT):
+        total += taps_ref[n, s : s + 1, lanes] * ext[n, s : s + ROWS, lanes]
+    return total.astype(BF16)
+
+
+def finish_kernel(
+    ext, taps_ref, att, qg, raw_ref, factor_ref, att_hbm, qg_hbm, kg_hbm, vg_hbm, fg_hbm,
+    fg_ref, grads, sems
+):
+    copies = [
+        pltpu.make_async_copy(att, att_hbm, sems.at[0]),
+        pltpu.make_async_copy(qg, qg_hbm, sems.at[1]),
+        pltpu.make_async_copy(fg_ref, fg_hbm, sems.at[2]),
+    ]
+    copies[0].start()
+    copies[1].start()
+    fg_ref[...] = raw_ref[...] * factor_ref[0:1]
+    copies[2].start()
+    for n, out in enumerate((kg_hbm, vg_hbm)):
+        for part in range(2):
+            for step in range(4):
+                lanes = slice(part * 512 + step * 128, part * 512 + step * 128 + 128)
+                grads[n, :, lanes] = anti_short(ext, taps_ref, n + 1, lanes)
+            lanes = slice(part * 512, part * 512 + 512)
+            at = 3 + 2 * n + part
+            copies.append(
+                pltpu.make_async_copy(grads.at[n, :, lanes], out.at[:, lanes], sems.at[at])
+            )
+            copies[-1].start()
+    for copy in copies:
+        copy.wait()
+
+
+def finish(ext, taps, att, qg, raw, factor):
+    wide = jax.ShapeDtypeStruct((ROWS, CHANNELS), BF16)
+    vmem = pl.BlockSpec(memory_space=pltpu.VMEM)
+    return pl.pallas_call(
+        finish_kernel,
+        out_shape=(wide, wide, wide, wide, jax.ShapeDtypeStruct((64, ROWS), F32)),
+        in_specs=[vmem] * 6,
+        out_specs=(pl.BlockSpec(memory_space=pltpu.HBM),) * 5,
+        scratch_shapes=[
+            pltpu.VMEM((64, ROWS), F32),
+            pltpu.VMEM((2, ROWS, CHANNELS), BF16),
+            pltpu.SemaphoreType.DMA((7,)),
+        ],
+        compiler_params=pltpu.CompilerParams(vmem_limit_bytes=6 * 1024 * 1024),
+    )(ext, taps, att, qg, raw, factor)
+
+
 def on_device(*args):
     vmem = pl.BlockSpec(memory_space=pltpu.VMEM)
+    anywhere = pl.BlockSpec(memory_space=pltpu.HBM)
+    own = pltpu.VMEM((ROWS, CHANNELS), BF16)
     wide = jax.ShapeDtypeStruct((ROWS, CHANNELS), BF16)
     exchanged = pltpu.VMEM((PEERS, NARROW, ROWS), BF16)
     half = SUPER * GROUP
-    return pl.pallas_call(
+    args = list(args)
+    taps = args[6]
+    args[7] = args[7].T
+    args = [pltpu.with_memory_space_constraint(arg, pltpu.HBM) for arg in args]
+    att, qg, ext, raw, factor = pl.pallas_call(
         kernel,
-        out_shape=(wide, wide, wide, wide, jax.ShapeDtypeStruct((ROWS, 64), F32)),
-        in_specs=[vmem] * 9,
+        out_shape=(
+            wide,
+            wide,
+            jax.ShapeDtypeStruct((3, ROWS + RIM, CHANNELS), F32),
+            jax.ShapeDtypeStruct((64, ROWS), F32),
+            jax.ShapeDtypeStruct((8, ROWS), F32),
+        ),
+        in_specs=[anywhere] * 9,
         out_specs=(vmem,) * 5,
         scratch_shapes=[
+            *[own] * 6,
+            pltpu.VMEM((3, SHORT, CHANNELS), F32),
+            pltpu.VMEM((64, ROWS), F32),
+            own,
+            pltpu.SemaphoreType.DMA((INPUTS,)),
             pltpu.VMEM((3 * RIM, CHANNELS), BF16),
             pltpu.VMEM((3 * RIM, CHANNELS), BF16),
             pltpu.VMEM((2, ROWS, CHANNELS), BF16),
-            pltpu.VMEM((3, ROWS + RIM, CHANNELS), F32),
             pltpu.VMEM((3, ROWS, CHANNELS), F32),
             pltpu.VMEM((PEERS, HELD, ROWS), F32),
             pltpu.VMEM((PEERS, HELD, ROWS), F32),
@@ -416,14 +524,14 @@
             pltpu.VMEM((TPS, 8, ROWS), F32),
             pltpu.VMEM((3, RIM, CHANNELS), BF16),
             pltpu.VMEM((3, RIM, CHANNELS), BF16),
-            pltpu.VMEM((2, PEERS + 8, ROWS), F32),
+            pltpu.VMEM((PEERS, 8, ROWS), F32),
             pltpu.VMEM((2 * half, 2 * ROWS), BF16),
             pltpu.VMEM((2 * half, 2 * ROWS), BF16),
             pltpu.VMEM((half, LONG), BF16),
             pltpu.VMEM((HELD, half, LONG), BF16),
             pltpu.VMEM((HELD, LONG + 256, 256), BF16),
             pltpu.VMEM((HELD, 256, LONG + 128), BF16),
-            pltpu.VMEM((2 * ROWS, LONG + ROWS), F32),
+            pltpu.VMEM((2 * ROWS, LONG + 2 * ROWS), F32),
             pltpu.SemaphoreType.DMA,
             pltpu.SemaphoreType.DMA,
             pltpu.SemaphoreType.DMA((2,)),
@@ -434,12 +542,14 @@
             pltpu.SemaphoreType.DMA((2,)),
         ],
         compiler_params=pltpu.CompilerParams(
-            collective_id=0, has_side_effects=True, vmem_limit_bytes=56 * 1024 * 1024
+            collective_id=0, has_side_effects=True, vmem_limit_bytes=32 * 1024 * 1024
         ),
         cost_estimate=pl.CostEstimate(
             flops=3_400_000_000, bytes_accessed=4_000_000, transcendentals=300_000
         ),
     )(*args)
+    outs = finish(ext, taps, att, qg, raw, factor)
+    return (*outs[:4], outs[4].T)
 
 
 def solution(mesh):

time: 64.8 us -> 56.7 us (0.88)
  local copies, waits for them, and re-layouts: 7.53 us -> 0.01 us
    unnamed x11 -> x2, local copies, waits for them, and re-layouts: 5.99 us -> 0.01 us
    pallas_call x1 -> x0, local copies, waits for them, and re-layouts: 1.54 us -> none  [on_device(): pl.pallas_call(kernel, out_shape=(wide, wide, wide, wide, jax.ShapeDtypeS...]
    pallas_call x1 -> x2, Pallas kernels: 56.3 us -> 55.9 us  [the longest x1 54.3 us: on_device(): pl.pallas_call(kernel, out_shape=(wide, wide, jax.ShapeDtypeStruct((3, RO...]
where the time goes in v1:
time: 56.7 us; the launch traced here: 56.6 us
  Pallas kernels  55.9 us (99%)
  between operations  0.66 us (1%)
    pallas_call x1, Pallas kernels, on_device(): pl.pallas_call(kernel, out_shape=(wide, wide, jax.ShapeDtypeStruct((3, RO...  54.3 us
    pallas_call x1, Pallas kernels, finish(): pl.pallas_call(finish_kernel, out_shape=(wide, wide, wide, wide, jax.Shap...  1.63 us

profile of v1, /device:TPU:1, one launch (start us, length us, event | category | flops | bytes accessed | tf_op | source)
XLA Modules:
  0.0 56.6 jit_solution(5656861482567226030)
XLA Ops:
  0.6 0.0 copy-start
  0.6 54.3 %shard_map.128 = (bf16[128,1024]{1,0:T(8,128)(2,1)S(1)}, bf16[128,1024]{1,0:T(8,128)(2,1)S(1)}, f32[3,144,1024]{2,1,0:T(8,128)S(1)}, f32[64,128]{1,0:T(8,128)S(1)}, f32[8,128]{1,0:T(8,128)S(1)}) custom-call(bf16[128,1024]{1,0:T(8,128)(2,1)} %q_hbm.1, bf16[128,1024]{1,0:T(8,128)(2,1)} %k_hbm.1, bf16[128,1024]{1,0:T(8,128)(2,1)} %v_hbm.1, ...), custom_call_target="tpu_custom_call" | custom-call | flops 3400000000 | bytes 4000000 | tf_op jit(solution)/shard_map/pallas_call | solution.py:497
  55.0 0.0 copy-done
  55.0 1.6 %shard_map.129 = (bf16[128,1024]{1,0:T(8,128)(2,1)}, bf16[128,1024]{1,0:T(8,128)(2,1)}, bf16[128,1024]{1,0:T(8,128)(2,1)}, bf16[128,1024]{1,0:T(8,128)(2,1)}, f32[64,128]{1,0:T(8,128)}) custom-call(f32[3,144,1024]{2,1,0:T(8,128)S(1)} %get-tuple-element.15.ext, f32[3,7,1024]{2,1,0:T(8,128)S(1)} %copy-done, bf16[128,1024]{1,0:T(8,128)(2,1)S(1)} %get-tuple-element.16.att, ...), custom_call_target="tpu_custom_call" | custom-call | tf_op jit(solution)/shard_map/pallas_call | solution.py:472
Async XLA Ops:
  0.6 54.3 %copy-start = (f32[3,7,1024]{2,1,0:T(8,128)S(1)}, f32[3,7,1024]{2,1,0:T(8,128)}, u32[]{:S(2)}) copy-start(f32[3,7,1024]{2,1,0:T(8,128)} %taps_ref.1) | copy-start | bytes 258052

commit v2 on v1

--- a/solution.py
+++ b/solution.py
@@ -46,7 +46,8 @@
     filt_hbm,
     up_hbm,
     att_ref,
-    qg_ref,
+    kg_ref,
+    vg_ref,
     ext,
     raw_ref,
     factor_ref,
@@ -107,10 +108,10 @@
 
     held = (q_ref, k_ref, v_ref, hq_ref, hk_ref, hv_ref, filt_ref, up_ref, taps_ref)
     loads = [pltpu.make_async_copy(hbm[n], held[n], load_sem.at[n]) for n in range(INPUTS)]
-    for n in (3, 4, 5, 6, 1, 2, 8, 7, 0):
+    for n in (3, 4, 5, 1):
         loads[n].start()
 
-    for step in STEPS:
+    for step in STEPS[::-1]:
         pl.semaphore_signal(
             barrier, inc=1, device_id=((me + step) % PEERS, tp), device_id_type=MESH
         )
@@ -119,18 +120,13 @@
             barrier, inc=1, device_id=(me, (tp + step) % TPS), device_id_type=MESH
         )
 
+    for n in (6, 8, 7, 2, 0):
+        loads[n].start()
     for n in (3, 4, 5):
         loads[n].wait()
     rim_out[0:RIM] = hq_ref[ROWS - RIM : ROWS]
     rim_out[RIM : 2 * RIM] = hk_ref[ROWS - RIM : ROWS]
     rim_out[2 * RIM : 3 * RIM] = hv_ref[ROWS - RIM : ROWS]
-    for n in range(3):
-        ext[n, RIM : RIM + ROWS] = held[3 + n][...].astype(F32)
-    loads[6].wait()
-    for p in range(PEERS):
-        send_h[p] = filt_ref[HELD * p : HELD * p + HELD]
-    loads[1].wait()
-    loads[2].wait()
     pl.semaphore_wait(barrier, PEERS - 1 + TPS - 1)
 
     def to_next(src, dst, send_sem, recv_sem, target):
@@ -161,24 +157,41 @@
         part = ref.at[pl.ds(0, PEERS - 1)]
         pltpu.make_async_copy(part, part, sem).wait()
 
+    loads[6].wait()
+    for p in range(PEERS):
+        send_h[p] = filt_ref[HELD * p : HELD * p + HELD]
+    scatter(send_h, recv_h, 0)
+    loads[1].wait()
     kv_copies = [
         to_next(src, kv_in.at[n], kv_send_sem.at[n], kv_recv_sem.at[n], after)
         for n, src in enumerate((k_ref, v_ref))
     ]
-    for copy in kv_copies:
-        copy.start()
-    scatter(send_h, recv_h, 0)
+    kv_copies[0].start()
+
+    for n in range(3):
+        ext[n, RIM : RIM + ROWS] = held[3 + n][...].astype(F32)
+        ext[n, 0:RIM] = jnp.zeros((RIM, CHANNELS), F32)
+    loads[8].wait()
+
+    def short_conv(n, rows, lanes):
+        total = taps_ref[n, 0:1, lanes] * ext[n, RIM : RIM + rows, lanes]
+        for s in range(1, SHORT):
+            total += taps_ref[n, s : s + 1, lanes] * ext[n, RIM - s : RIM - s + rows, lanes]
+        return total
+
+    @pl.loop(0, CHANNELS // 128)
+    def _(chunk):
+        lanes = pl.ds(pl.multiple_of(chunk * 128, 128), 128)
+        for n in range(3):
+            short[n, :, lanes] = short_conv(n, ROWS, lanes)
 
     rim_copy.wait_recv()
     for n in range(3):
         leading = rim_in[n * RIM : (n + 1) * RIM].astype(F32)
         ext[n, 0:RIM] = jnp.where(me > 0, leading, 0.0)
 
-    def short_conv(n, lanes):
-        total = taps_ref[n, 0:1, lanes] * ext[n, RIM : RIM + ROWS, lanes]
-        for s in range(1, SHORT):
-            total += taps_ref[n, s : s + 1, lanes] * ext[n, RIM - s : RIM - s + ROWS, lanes]
-        return total
+    for n in range(3):
+        short[n, 0:8] = short_conv(n, 8, slice(None))
 
     mine = me // 4
 
@@ -198,25 +211,23 @@
             send_one(src, dst, which, mine * 4 + (me + n) % 4)
         keep(src, dst)
 
+    def blocks_of(wide):
+        return wide.T.astype(BF16).reshape(4, NARROW, ROWS)
+
+    def delta_chunk(chunk):
+        lanes = pl.ds(pl.multiple_of(chunk * 128, 128), 128)
+        send_g[pl.ds(chunk * 4, 4)] = blocks_of(up_ref[:, lanes].astype(F32) * short[0, :, lanes])
+
     def mixed_chunk(chunk):
         lanes = pl.ds(pl.multiple_of(chunk * 128, 128), 128)
-        short_k = short_conv(1, lanes)
-        short_v = short_conv(2, lanes)
-        short[1, :, lanes] = short_k
-        short[2, :, lanes] = short_v
-        mixed = (short_k * short_v).T.astype(BF16)
-        send_m[pl.ds(chunk * 4, 4)] = mixed.reshape(4, NARROW, ROWS)
-
-    def delta_chunk(chunk):
-        lanes = pl.ds(pl.multiple_of(chunk * 128, 128), 128)
-        delta = (up_ref[:, lanes].astype(F32) * short_conv(0, lanes)).T.astype(BF16)
-        send_g[pl.ds(chunk * 4, 4)] = delta.reshape(4, NARROW, ROWS)
-
-    loads[8].wait()
-    by_chunk(mixed_chunk, send_m, recv_m, 1)
+        send_m[pl.ds(chunk * 4, 4)] = blocks_of(short[1, :, lanes] * short[2, :, lanes])
+
     loads[7].wait()
     by_chunk(delta_chunk, send_g, recv_g, 2)
-
+    loads[2].wait()
+    by_chunk(mixed_chunk, send_m, recv_m, 1)
+
+    kv_copies[1].start()
     row_at = lax.broadcasted_iota(jnp.int32, (ROWS, ROWS), 0)
     lane_at = lax.broadcasted_iota(jnp.int32, (ROWS, ROWS), 1)
     settle(recv_h, in_sem.at[0])
@@ -265,6 +276,18 @@
         )
         send[:, g * GROUP : (g + 1) * GROUP, :] = both.reshape(PEERS, GROUP, ROWS)
 
+    settle(recv_g, in_sem.at[2])
+    padded_g[half : 2 * half] = jnp.zeros((half, 2 * ROWS), BF16)
+    for g in range(HELD):
+        even, odd = paired(recv_g, g)
+        padded_g[0:half, 0:ROWS] = even
+        padded_g[0:half, ROWS : 2 * ROWS] = odd
+        for d in range(SUPER):
+            left_g[g, :, d * 256 : (d + 1) * 256] = padded_g[GROUP * d : half + GROUP * d]
+        back = dot(left_g[g], weight_d[g, :, 0:LONG], ((1,), (1,))).astype(BF16)
+        spread(send_d, back, g)
+    scatter(send_d, recv_d, 4)
+
     settle(recv_m, in_sem.at[1])
     padded_m[0:half] = jnp.zeros((half, 2 * ROWS), BF16)
     for g in range(HELD):
@@ -276,18 +299,6 @@
         conv = dot(left_m[...], weight_c[g, 0:LONG], ((1,), (0,))).astype(BF16)
         spread(send_c, conv, g)
     scatter(send_c, recv_c, 3)
-
-    settle(recv_g, in_sem.at[2])
-    padded_g[half : 2 * half] = jnp.zeros((half, 2 * ROWS), BF16)
-    for g in range(HELD):
-        even, odd = paired(recv_g, g)
-        padded_g[0:half, 0:ROWS] = even
-        padded_g[0:half, ROWS : 2 * ROWS] = odd
-        for d in range(SUPER):
-            left_g[g, :, d * 256 : (d + 1) * 256] = padded_g[GROUP * d : half + GROUP * d]
-        back = dot(left_g[g], weight_d[g, :, 0:LONG], ((1,), (1,))).astype(BF16)
-        spread(send_d, back, g)
-    scatter(send_d, recv_d, 4)
 
     reversal = (row_at + lane_at == ROWS - 1).astype(BF16)
     upper = (lane_at < row_at) | (lane_at == ROWS - 1)
@@ -372,17 +383,6 @@
         trailing = edge_in[n].astype(F32)
         ext[n, ROWS : ROWS + RIM] = jnp.where(me < PEERS - 1, trailing, 0.0)
 
-    settle(recv_c, in_sem.at[3])
-    follow(0, recv_c)
-    edge_copy(0).start()
-    edge_copy(0).wait_recv()
-    trail(0)
-
-    @pl.loop(0, CHANNELS // 128)
-    def _(chunk):
-        lanes = pl.ds(pl.multiple_of(chunk * 128, 128), 128)
-        qg_ref[:, lanes] = anti_short(ext, taps_ref, 0, lanes)
-
     settle(recv_d, in_sem.at[4])
     follow(1, recv_d)
     edge_copy(1).start()
@@ -402,24 +402,35 @@
             device_id_type=MESH,
         )
 
-    @pl.loop(1, TPS)
-    def _(step):
+    for step in range(1, TPS):
         norm_copy(step).start()
-
     recv_n[pl.ds(tp, 1)] = send_n[...].reshape(1, 8, ROWS)
-
     for p in range(PEERS):
         raw_ref[HELD * p : HELD * p + HELD] = recv_f[p, 0:HELD]
+
     edge_copy(1).wait_recv()
     trail(1)
     trail(2)
 
+    @pl.loop(0, CHANNELS // 128)
+    def _(chunk):
+        lanes = pl.ds(pl.multiple_of(chunk * 128, 128), 128)
+        kg_ref[:, lanes] = anti_short(ext, taps_ref, 1, lanes)
+        vg_ref[:, lanes] = anti_short(ext, taps_ref, 2, lanes)
+
+    settle(recv_c, in_sem.at[3])
+    follow(0, recv_c)
+    edge_copy(0).start()
     part = recv_n.at[pl.ds(0, TPS - 1)]
     pltpu.make_async_copy(part, part, in_sem.at[6]).wait()
     total = jnp.sum(recv_n[:, 0, :], axis=0, keepdims=True)
     total = jnp.sum(total, axis=1, keepdims=True)
     factor = jnp.minimum(1.0, math.sqrt(TOTAL) / jnp.sqrt(total))
     factor_ref[...] = jnp.broadcast_to(factor, (8, ROWS))
+
+
+    edge_copy(0).wait_recv()
+    trail(0)
 
     rim_copy.wait_send()
     for copy in kv_copies:
@@ -439,48 +450,47 @@
 
 
 def finish_kernel(
-    ext, taps_ref, att, qg, raw_ref, factor_ref, att_hbm, qg_hbm, kg_hbm, vg_hbm, fg_hbm,
+    ext, taps_ref, att, kg, vg, raw_ref, factor_ref, att_hbm, qg_hbm, kg_hbm, vg_hbm, fg_hbm,
     fg_ref, grads, sems
 ):
     copies = [
         pltpu.make_async_copy(att, att_hbm, sems.at[0]),
-        pltpu.make_async_copy(qg, qg_hbm, sems.at[1]),
-        pltpu.make_async_copy(fg_ref, fg_hbm, sems.at[2]),
+        pltpu.make_async_copy(kg, kg_hbm, sems.at[1]),
+        pltpu.make_async_copy(vg, vg_hbm, sems.at[2]),
+        pltpu.make_async_copy(fg_ref, fg_hbm, sems.at[3]),
     ]
-    copies[0].start()
-    copies[1].start()
+    for copy in copies[:3]:
+        copy.start()
     fg_ref[...] = raw_ref[...] * factor_ref[0:1]
-    copies[2].start()
-    for n, out in enumerate((kg_hbm, vg_hbm)):
-        for part in range(2):
-            for step in range(4):
-                lanes = slice(part * 512 + step * 128, part * 512 + step * 128 + 128)
-                grads[n, :, lanes] = anti_short(ext, taps_ref, n + 1, lanes)
-            lanes = slice(part * 512, part * 512 + 512)
-            at = 3 + 2 * n + part
-            copies.append(
-                pltpu.make_async_copy(grads.at[n, :, lanes], out.at[:, lanes], sems.at[at])
-            )
-            copies[-1].start()
+    copies[3].start()
+    for part in range(4):
+        for step in range(2):
+            lanes = slice(part * 256 + step * 128, part * 256 + step * 128 + 128)
+            grads[:, lanes] = anti_short(ext, taps_ref, 0, lanes)
+        lanes = slice(part * 256, part * 256 + 256)
+        copies.append(
+            pltpu.make_async_copy(grads.at[:, lanes], qg_hbm.at[:, lanes], sems.at[4 + part])
+        )
+        copies[-1].start()
     for copy in copies:
         copy.wait()
 
 
-def finish(ext, taps, att, qg, raw, factor):
+def finish(*args):
     wide = jax.ShapeDtypeStruct((ROWS, CHANNELS), BF16)
     vmem = pl.BlockSpec(memory_space=pltpu.VMEM)
     return pl.pallas_call(
         finish_kernel,
         out_shape=(wide, wide, wide, wide, jax.ShapeDtypeStruct((64, ROWS), F32)),
-        in_specs=[vmem] * 6,
+        in_specs=[vmem] * 7,
         out_specs=(pl.BlockSpec(memory_space=pltpu.HBM),) * 5,
         scratch_shapes=[
             pltpu.VMEM((64, ROWS), F32),
-            pltpu.VMEM((2, ROWS, CHANNELS), BF16),
-            pltpu.SemaphoreType.DMA((7,)),
+            pltpu.VMEM((ROWS, CHANNELS), BF16),
+            pltpu.SemaphoreType.DMA((8,)),
         ],
         compiler_params=pltpu.CompilerParams(vmem_limit_bytes=6 * 1024 * 1024),
-    )(ext, taps, att, qg, raw, factor)
+    )(*args)
 
 
 def on_device(*args):
@@ -494,9 +504,10 @@
     taps = args[6]
     args[7] = args[7].T
     args = [pltpu.with_memory_space_constraint(arg, pltpu.HBM) for arg in args]
-    att, qg, ext, raw, factor = pl.pallas_call(
+    att, kg, vg, ext, raw, factor = pl.pallas_call(
         kernel,
         out_shape=(
+            wide,
             wide,
             wide,
             jax.ShapeDtypeStruct((3, ROWS + RIM, CHANNELS), F32),
@@ -504,7 +515,7 @@
             jax.ShapeDtypeStruct((8, ROWS), F32),
         ),
         in_specs=[anywhere] * 9,
-        out_specs=(vmem,) * 5,
+        out_specs=(vmem,) * 6,
         scratch_shapes=[
             *[own] * 6,
             pltpu.VMEM((3, SHORT, CHANNELS), F32),
@@ -548,7 +559,7 @@
             flops=3_400_000_000, bytes_accessed=4_000_000, transcendentals=300_000
         ),
     )(*args)
-    outs = finish(ext, taps, att, qg, raw, factor)
+    outs = finish(ext, taps, att, kg, vg, raw, factor)
     return (*outs[:4], outs[4].T)
 
 

time: 56.7 us -> 52.7 us (0.929)
  Pallas kernels: 55.9 us -> 51.9 us
    pallas_call x1, Pallas kernels: 54.3 us -> 50.7 us  [on_device(): pl.pallas_call(kernel, out_shape=(wide, wide, wide, jax.ShapeDtypeStruct(...]
where the time goes in v2:
time: 52.7 us; the launch traced here: 52.5 us
  Pallas kernels  51.9 us (98%)
  between operations  0.66 us (1%)
    pallas_call x1, Pallas kernels, on_device(): pl.pallas_call(kernel, out_shape=(wide, wide, wide, jax.ShapeDtypeStruct(...  50.7 us
    pallas_call x1, Pallas kernels, finish(): pl.pallas_call(finish_kernel, out_shape=(wide, wide, wide, wide, jax.Shap...  1.16 us

profile of v2, /device:TPU:1, one launch (start us, length us, event | category | flops | bytes accessed | tf_op | source)
XLA Modules:
  0.0 52.5 jit_solution(7244303803374243778)
XLA Ops:
  0.6 0.0 copy-start
  0.6 50.7 %shard_map.128 = (bf16[128,1024]{1,0:T(8,128)(2,1)S(1)}, bf16[128,1024]{1,0:T(8,128)(2,1)S(1)}, bf16[128,1024]{1,0:T(8,128)(2,1)S(1)}, f32[3,144,1024]{2,1,0:T(8...) custom-call(bf16[128,1024]{1,0:T(8,128)(2,1)} %q_hbm.1, bf16[128,1024]{1,0:T(8,128)(2,1)} %k_hbm.1, ...), custom_call_target="tpu_custom_call" | custom-call | flops 3400000000 | bytes 4000000 | tf_op jit(solution)/shard_map/pallas_call | solution.py:507
  51.4 0.0 copy-done
  51.4 1.2 %shard_map.129 = (bf16[128,1024]{1,0:T(8,128)(2,1)}, bf16[128,1024]{1,0:T(8,128)(2,1)}, bf16[128,1024]{1,0:T(8,128)(2,1)}, bf16[128,1024]{1,0:T(8,128)(2,1)}, f32[64,128]{1,0:T(8,128)}) custom-call(f32[3,144,1024]{2,1,0:T(8,128)S(1)} %get-tuple-element.16.ext, f32[3,7,1024]{2,1,0:T(8,128)S(1)} %copy-done, bf16[128,1024]{1,0:T(8,128)(2,1)S(1)} %get-tuple-element.17.att, ...), custom_call_target="tpu_custom_call" | custom-call | tf_op jit(solution)/shard_map/pallas_call | solution.py:482
Async XLA Ops:
  0.6 50.7 %copy-start = (f32[3,7,1024]{2,1,0:T(8,128)S(1)}, f32[3,7,1024]{2,1,0:T(8,128)}, u32[]{:S(2)}) copy-start(f32[3,7,1024]{2,1,0:T(8,128)} %taps_ref.1) | copy-start | bytes 258052

commit v3 on v2

--- a/solution.py
+++ b/solution.py
@@ -355,7 +355,7 @@
         attend(2 * pair + 1)
 
     def follow(n, source):
-        def chunk_step(chunk, carry):
+        def chunk_step(chunk):
             lanes = pl.ds(pl.multiple_of(chunk * 128, 128), 128)
             part = source[pl.ds(chunk * 4, 4)].reshape(4 * NARROW, ROWS).astype(F32).T
             if n == 0:
@@ -365,9 +365,11 @@
             for which, grad in grads:
                 ext[which, 0:ROWS, lanes] = grad
                 edge_out[which, :, lanes] = grad[0:RIM].astype(BF16)
-            return carry
-
-        lax.fori_loop(0, CHANNELS // 128, chunk_step, 0)
+
+        @pl.loop(0, CHANNELS // 256)
+        def _(pair):
+            chunk_step(2 * pair)
+            chunk_step(2 * pair + 1)
 
     def edge_copy(n):
         part = pl.ds(0, 1) if n == 0 else pl.ds(1, 2)
@@ -408,6 +410,9 @@
     for p in range(PEERS):
         raw_ref[HELD * p : HELD * p + HELD] = recv_f[p, 0:HELD]
 
+    settle(recv_c, in_sem.at[3])
+    follow(0, recv_c)
+    edge_copy(0).start()
     edge_copy(1).wait_recv()
     trail(1)
     trail(2)
@@ -418,9 +423,6 @@
         kg_ref[:, lanes] = anti_short(ext, taps_ref, 1, lanes)
         vg_ref[:, lanes] = anti_short(ext, taps_ref, 2, lanes)
 
-    settle(recv_c, in_sem.at[3])
-    follow(0, recv_c)
-    edge_copy(0).start()
     part = recv_n.at[pl.ds(0, TPS - 1)]
     pltpu.make_async_copy(part, part, in_sem.at[6]).wait()
     total = jnp.sum(recv_n[:, 0, :], axis=0, keepdims=True)

time: 52.7 us -> 51.6 us (0.979)
  Pallas kernels: 51.9 us -> 50.8 us
    pallas_call x1, Pallas kernels: 50.7 us -> 49.6 us  [on_device(): pl.pallas_call(kernel, out_shape=(wide, wide, wide, jax.ShapeDtypeStruct(...]
where the time goes in v3:
time: 51.6 us; the launch traced here: 51.5 us
  Pallas kernels  50.8 us (98%)
  between operations  0.66 us (1%)
    pallas_call x1, Pallas kernels, on_device(): pl.pallas_call(kernel, out_shape=(wide, wide, wide, jax.ShapeDtypeStruct(...  49.6 us
    pallas_call x1, Pallas kernels, finish(): pl.pallas_call(finish_kernel, out_shape=(wide, wide, wide, wide, jax.Shap...  1.16 us

profile of v3, /device:TPU:1, one launch (start us, length us, event | category | flops | bytes accessed | tf_op | source)
XLA Modules:
  0.0 51.5 jit_solution(4332881499602193343)
XLA Ops:
  0.6 0.0 copy-start
  0.6 49.6 %shard_map.128 = (bf16[128,1024]{1,0:T(8,128)(2,1)S(1)}, bf16[128,1024]{1,0:T(8,128)(2,1)S(1)}, bf16[128,1024]{1,0:T(8,128)(2,1)S(1)}, f32[3,144,1024]{2,1,0:T(8...) custom-call(bf16[128,1024]{1,0:T(8,128)(2,1)} %q_hbm.1, bf16[128,1024]{1,0:T(8,128)(2,1)} %k_hbm.1, ...), custom_call_target="tpu_custom_call" | custom-call | flops 3400000000 | bytes 4000000 | tf_op jit(solution)/shard_map/pallas_call | solution.py:509
  50.3 0.0 copy-done
  50.3 1.2 %shard_map.129 = (bf16[128,1024]{1,0:T(8,128)(2,1)}, bf16[128,1024]{1,0:T(8,128)(2,1)}, bf16[128,1024]{1,0:T(8,128)(2,1)}, bf16[128,1024]{1,0:T(8,128)(2,1)}, f32[64,128]{1,0:T(8,128)}) custom-call(f32[3,144,1024]{2,1,0:T(8,128)S(1)} %get-tuple-element.16.ext, f32[3,7,1024]{2,1,0:T(8,128)S(1)} %copy-done, bf16[128,1024]{1,0:T(8,128)(2,1)S(1)} %get-tuple-element.17.att, ...), custom_call_target="tpu_custom_call" | custom-call | tf_op jit(solution)/shard_map/pallas_call | solution.py:484
Async XLA Ops:
  0.6 49.7 %copy-start = (f32[3,7,1024]{2,1,0:T(8,128)S(1)}, f32[3,7,1024]{2,1,0:T(8,128)}, u32[]{:S(2)}) copy-start(f32[3,7,1024]{2,1,0:T(8,128)} %taps_ref.1) | copy-start | bytes 258052

commit v4 on v3

--- a/solution.py
+++ b/solution.py
@@ -108,9 +108,6 @@
 
     held = (q_ref, k_ref, v_ref, hq_ref, hk_ref, hv_ref, filt_ref, up_ref, taps_ref)
     loads = [pltpu.make_async_copy(hbm[n], held[n], load_sem.at[n]) for n in range(INPUTS)]
-    for n in (3, 4, 5, 1):
-        loads[n].start()
-
     for step in STEPS[::-1]:
         pl.semaphore_signal(
             barrier, inc=1, device_id=((me + step) % PEERS, tp), device_id_type=MESH
@@ -120,13 +117,29 @@
             barrier, inc=1, device_id=(me, (tp + step) % TPS), device_id_type=MESH
         )
 
-    for n in (6, 8, 7, 2, 0):
+    for n in (3, 4, 5, 1, 6, 8, 7, 2, 0):
         loads[n].start()
     for n in (3, 4, 5):
         loads[n].wait()
     rim_out[0:RIM] = hq_ref[ROWS - RIM : ROWS]
     rim_out[RIM : 2 * RIM] = hk_ref[ROWS - RIM : ROWS]
     rim_out[2 * RIM : 3 * RIM] = hv_ref[ROWS - RIM : ROWS]
+    for n in range(3):
+        ext[n, RIM : RIM + ROWS] = held[3 + n][...].astype(F32)
+        ext[n, 0:RIM] = jnp.zeros((RIM, CHANNELS), F32)
+    loads[8].wait()
+
+    def short_conv(n, rows, lanes):
+        total = taps_ref[n, 0:1, lanes] * ext[n, RIM : RIM + rows, lanes]
+        for s in range(1, SHORT):
+            total += taps_ref[n, s : s + 1, lanes] * ext[n, RIM - s : RIM - s + rows, lanes]
+        return total
+
+    @pl.loop(0, CHANNELS // 128)
+    def _(chunk):
+        lanes = pl.ds(pl.multiple_of(chunk * 128, 128), 128)
+        short[0, :, lanes] = short_conv(0, ROWS, lanes)
+
     pl.semaphore_wait(barrier, PEERS - 1 + TPS - 1)
 
     def to_next(src, dst, send_sem, recv_sem, target):
@@ -168,30 +181,12 @@
     ]
     kv_copies[0].start()
 
-    for n in range(3):
-        ext[n, RIM : RIM + ROWS] = held[3 + n][...].astype(F32)
-        ext[n, 0:RIM] = jnp.zeros((RIM, CHANNELS), F32)
-    loads[8].wait()
-
-    def short_conv(n, rows, lanes):
-        total = taps_ref[n, 0:1, lanes] * ext[n, RIM : RIM + rows, lanes]
-        for s in range(1, SHORT):
-            total += taps_ref[n, s : s + 1, lanes] * ext[n, RIM - s : RIM - s + rows, lanes]
-        return total
-
-    @pl.loop(0, CHANNELS // 128)
-    def _(chunk):
-        lanes = pl.ds(pl.multiple_of(chunk * 128, 128), 128)
-        for n in range(3):
-            short[n, :, lanes] = short_conv(n, ROWS, lanes)
-
     rim_copy.wait_recv()
     for n in range(3):
         leading = rim_in[n * RIM : (n + 1) * RIM].astype(F32)
         ext[n, 0:RIM] = jnp.where(me > 0, leading, 0.0)
 
-    for n in range(3):
-        short[n, 0:8] = short_conv(n, 8, slice(None))
+    short[0, 0:8] = short_conv(0, 8, slice(None))
 
     mine = me // 4
 
@@ -220,6 +215,8 @@
 
     def mixed_chunk(chunk):
         lanes = pl.ds(pl.multiple_of(chunk * 128, 128), 128)
+        for n in (1, 2):
+            short[n, :, lanes] = short_conv(n, ROWS, lanes)
         send_m[pl.ds(chunk * 4, 4)] = blocks_of(short[1, :, lanes] * short[2, :, lanes])
 
     loads[7].wait()

time: 51.6 us -> 51.6 us (level)
  no operation moved by 1% of the time
where the time goes in v4:
time: 51.6 us; the launch traced here: 51.5 us
  Pallas kernels  50.8 us (98%)
  between operations  0.66 us (1%)
    pallas_call x1, Pallas kernels, on_device(): pl.pallas_call(kernel, out_shape=(wide, wide, wide, jax.ShapeDtypeStruct(...  49.6 us
    pallas_call x1, Pallas kernels, finish(): pl.pallas_call(finish_kernel, out_shape=(wide, wide, wide, wide, jax.Shap...  1.16 us

profile of v4, /device:TPU:1, one launch (start us, length us, event | category | flops | bytes accessed | tf_op | source)
XLA Modules:
  0.0 51.5 jit_solution(9185265018349852272)
XLA Ops:
  0.6 0.0 copy-start
  0.6 49.6 %shard_map.128 = (bf16[128,1024]{1,0:T(8,128)(2,1)S(1)}, bf16[128,1024]{1,0:T(8,128)(2,1)S(1)}, bf16[128,1024]{1,0:T(8,128)(2,1)S(1)}, f32[3,144,1024]{2,1,0:T(8...) custom-call(bf16[128,1024]{1,0:T(8,128)(2,1)} %q_hbm.1, bf16[128,1024]{1,0:T(8,128)(2,1)} %k_hbm.1, ...), custom_call_target="tpu_custom_call" | custom-call | flops 3400000000 | bytes 4000000 | tf_op jit(solution)/shard_map/pallas_call | solution.py:506
  50.3 0.0 copy-done
  50.3 1.2 %shard_map.129 = (bf16[128,1024]{1,0:T(8,128)(2,1)}, bf16[128,1024]{1,0:T(8,128)(2,1)}, bf16[128,1024]{1,0:T(8,128)(2,1)}, bf16[128,1024]{1,0:T(8,128)(2,1)}, f32[64,128]{1,0:T(8,128)}) custom-call(f32[3,144,1024]{2,1,0:T(8,128)S(1)} %get-tuple-element.16.ext, f32[3,7,1024]{2,1,0:T(8,128)S(1)} %copy-done, bf16[128,1024]{1,0:T(8,128)(2,1)S(1)} %get-tuple-element.17.att, ...), custom_call_target="tpu_custom_call" | custom-call | tf_op jit(solution)/shard_map/pallas_call | solution.py:481
Async XLA Ops:
  0.6 49.7 %copy-start = (f32[3,7,1024]{2,1,0:T(8,128)S(1)}, f32[3,7,1024]{2,1,0:T(8,128)}, u32[]{:S(2)}) copy-start(f32[3,7,1024]{2,1,0:T(8,128)} %taps_ref.1) | copy-start | bytes 258052

commit v5 on v4

--- a/solution.py
+++ b/solution.py
@@ -326,31 +326,6 @@
         )
     scatter(send_f, recv_f, 5)
 
-    for copy in kv_copies:
-        copy.wait_recv()
-    query_at = lax.broadcasted_iota(jnp.int32, (ROWS, 2 * ROWS), 0)
-    key_at = lax.broadcasted_iota(jnp.int32, (ROWS, 2 * ROWS), 1) - ROWS
-    first = jnp.where(me > 0, -ROWS, 0)
-    allowed = (key_at <= query_at) & (key_at >= first)
-
-    loads[0].wait()
-
-    def attend(head):
-        lanes = pl.ds(pl.multiple_of(head * HEAD_DIM, HEAD_DIM), HEAD_DIM)
-        keys = jnp.concatenate([kv_in[0, :, lanes], k_ref[:, lanes]], 0)
-        values = jnp.concatenate([kv_in[1, :, lanes], v_ref[:, lanes]], 0)
-        scores = dot(q_ref[:, lanes], keys, ((1,), (1,))) * (1.0 / math.sqrt(HEAD_DIM))
-        masked = jnp.where(allowed, scores, -jnp.inf)
-        largest = jnp.max(masked, axis=1, keepdims=True)
-        raised = jnp.exp(masked - largest)
-        weights = (raised / jnp.sum(raised, axis=1, keepdims=True)).astype(BF16)
-        att_ref[:, lanes] = dot(weights, values, ((1,), (0,))).astype(BF16)
-
-    @pl.loop(0, CHANNELS // HEAD_DIM // 2)
-    def _(pair):
-        attend(2 * pair)
-        attend(2 * pair + 1)
-
     def follow(n, source):
         def chunk_step(chunk):
             lanes = pl.ds(pl.multiple_of(chunk * 128, 128), 128)
@@ -385,6 +360,32 @@
     settle(recv_d, in_sem.at[4])
     follow(1, recv_d)
     edge_copy(1).start()
+
+    for copy in kv_copies:
+        copy.wait_recv()
+    query_at = lax.broadcasted_iota(jnp.int32, (ROWS, 2 * ROWS), 0)
+    key_at = lax.broadcasted_iota(jnp.int32, (ROWS, 2 * ROWS), 1) - ROWS
+    first = jnp.where(me > 0, -ROWS, 0)
+    allowed = (key_at <= query_at) & (key_at >= first)
+
+    loads[0].wait()
+
+    def attend(head):
+        lanes = pl.ds(pl.multiple_of(head * HEAD_DIM, HEAD_DIM), HEAD_DIM)
+        keys = jnp.concatenate([kv_in[0, :, lanes], k_ref[:, lanes]], 0)
+        values = jnp.concatenate([kv_in[1, :, lanes], v_ref[:, lanes]], 0)
+        scores = dot(q_ref[:, lanes], keys, ((1,), (1,))) * (1.0 / math.sqrt(HEAD_DIM))
+        masked = jnp.where(allowed, scores, -jnp.inf)
+        largest = jnp.max(masked, axis=1, keepdims=True)
+        raised = jnp.exp(masked - largest)
+        weights = (raised / jnp.sum(raised, axis=1, keepdims=True)).astype(BF16)
+        att_ref[:, lanes] = dot(weights, values, ((1,), (0,))).astype(BF16)
+
+    @pl.loop(0, CHANNELS // HEAD_DIM // 2)
+    def _(pair):
+        attend(2 * pair)
+        attend(2 * pair + 1)
+
 
     settle(recv_f, in_sem.at[5])
     squares = jnp.sum(recv_f[:, HELD : 2 * HELD, :], axis=0)

time: 51.6 us -> 51.6 us (level)
  no operation moved by 1% of the time
where the time goes in v5:
time: 51.6 us; the launch traced here: 51.5 us
  Pallas kernels  50.8 us (98%)
  between operations  0.66 us (1%)
    pallas_call x1, Pallas kernels, on_device(): pl.pallas_call(kernel, out_shape=(wide, wide, wide, jax.ShapeDtypeStruct(...  49.6 us
    pallas_call x1, Pallas kernels, finish(): pl.pallas_call(finish_kernel, out_shape=(wide, wide, wide, wide, jax.Shap...  1.16 us

profile of v5, /device:TPU:1, one launch (start us, length us, event | category | flops | bytes accessed | tf_op | source)
XLA Modules:
  0.0 51.5 jit_solution(14199212440437938729)
XLA Ops:
  0.6 0.0 copy-start
  0.6 49.6 %shard_map.128 = (bf16[128,1024]{1,0:T(8,128)(2,1)S(1)}, bf16[128,1024]{1,0:T(8,128)(2,1)S(1)}, bf16[128,1024]{1,0:T(8,128)(2,1)S(1)}, f32[3,144,1024]{2,1,0:T(8...) custom-call(bf16[128,1024]{1,0:T(8,128)(2,1)} %q_hbm.1, bf16[128,1024]{1,0:T(8,128)(2,1)} %k_hbm.1, ...), custom_call_target="tpu_custom_call" | custom-call | flops 3400000000 | bytes 4000000 | tf_op jit(solution)/shard_map/pallas_call | solution.py:507
  50.3 0.0 copy-done
  50.3 1.2 %shard_map.129 = (bf16[128,1024]{1,0:T(8,128)(2,1)}, bf16[128,1024]{1,0:T(8,128)(2,1)}, bf16[128,1024]{1,0:T(8,128)(2,1)}, bf16[128,1024]{1,0:T(8,128)(2,1)}, f32[64,128]{1,0:T(8,128)}) custom-call(f32[3,144,1024]{2,1,0:T(8,128)S(1)} %get-tuple-element.16.ext, f32[3,7,1024]{2,1,0:T(8,128)S(1)} %copy-done, bf16[128,1024]{1,0:T(8,128)(2,1)S(1)} %get-tuple-element.17.att, ...), custom_call_target="tpu_custom_call" | custom-call | tf_op jit(solution)/shard_map/pallas_call | solution.py:482
Async XLA Ops:
  0.6 49.7 %copy-start = (f32[3,7,1024]{2,1,0:T(8,128)S(1)}, f32[3,7,1024]{2,1,0:T(8,128)}, u32[]{:S(2)}) copy-start(f32[3,7,1024]{2,1,0:T(8,128)} %taps_ref.1) | copy-start | bytes 258052
